TPU v7x, 32 devices: a whole 2x2x4 slice. The times are simulated.
32 devices in a mesh: cuts: 4 (over z), amp: 8 (over y, x, core).
Axes of the slice: x: 2, y: 2, z: 4, core: 2. Of those that a mesh axis runs over, the one named last changes fastest.
Arguments:
- stem_state: bfloat16 [8, 32, 8, 128, 256], P('cuts', None, 'amp'), may hold values from -6 to 6
- gates: bfloat16 [8, 4, 2, 128, 128], P('cuts'), may hold values from -0.375 to 0.375
Outputs:
- amplitudes: float32 [32, 8, 128, 256], P('cuts', 'amp')
All inputs are finite; a program needn't handle non-finite values.
Results may differ from a plain program's by a relative error of at most 0.0049.
Values may be sent and summed in bfloat16 or wider, within the bound.
A program may use at most 64 MiB of HBM per device.

v0:
```python
import jax
import jax.numpy as jnp
from jax import lax
from jax.sharding import PartitionSpec as P


def block_matrix(gate):
    real_part = gate[0]
    imag_part = gate[1]
    top = jnp.concatenate([real_part.T, imag_part.T], axis=1)
    bottom = jnp.concatenate([-imag_part.T, real_part.T], axis=1)
    return jnp.concatenate([top, bottom], axis=0)


def on_rows(values, real_gates, imag_gates):
    width = values.shape[-1] // 2
    first_term = jnp.einsum(
        "ska,shgac->shgkc", real_gates, values, preferred_element_type=jnp.float32
    )
    second_term = jnp.einsum(
        "ska,shgac->shgkc", imag_gates, values, preferred_element_type=jnp.float32
    )
    real_out = first_term[..., :width] - second_term[..., width:]
    imag_out = first_term[..., width:] + second_term[..., :width]
    return jnp.concatenate([real_out, imag_out], axis=-1)


def on_last(values, matrices):
    return jnp.einsum("shgac,scd->shgad", values, matrices, preferred_element_type=jnp.float32)


def per_device(stem_state, gates):
    groups = lax.axis_size("amp")
    slice_count, hidden, single, width, columns = stem_state.shape
    low = width // groups
    first = on_rows(stem_state, gates[:, 0, 0], gates[:, 0, 1]).astype(jnp.bfloat16)
    second_matrix = jax.vmap(block_matrix)(gates[:, 1])
    second = on_last(first, second_matrix).astype(jnp.bfloat16)
    split_state = second.reshape(slice_count, hidden, 1, groups, low, columns)
    last_matrix = jax.vmap(block_matrix)(gates[:, 3])
    pieces = lax.all_to_all(split_state, "amp", split_axis=3, concat_axis=2, tiled=True)
    count = pieces.shape[1]
    merged = pieces.reshape(slice_count, count, 1, width, columns)
    third = on_rows(merged, gates[:, 2, 0], gates[:, 2, 1]).astype(jnp.bfloat16)
    fourth = on_last(third, last_matrix).reshape(slice_count, count, width, columns)
    total = jnp.sum(fourth, axis=0)
    summed = lax.psum_scatter(total, "cuts", scatter_dimension=0, tiled=True)
    share = summed.shape[0]
    outgoing = summed.reshape(share, groups, 1, low, columns)
    owned = lax.all_to_all(outgoing, "amp", split_axis=1, concat_axis=2, tiled=True)
    return owned.reshape(share, 1, width, columns)


def solution(mesh):
    placed = (P("cuts", None, "amp", None, None), P("cuts", None, None, None, None))
    return jax.shard_map(
        per_device,
        mesh=mesh,
        in_specs=placed,
        out_specs=P("cuts", "amp", None, None),
        check_vma=False,
    )
```

profile of v0, /device:TPU:0, one launch (start us, length us, event | category | flops | bytes accessed | tf_op | source)
XLA Modules:
  0.0 201.2 jit_solution(5708273051918047746)
XLA Ops:
  6.5 0.0 copy-start
  6.5 0.0 copy-start.1
  6.5 7.3 %fusion.19 = f32[2,32,1,128,256]{3,4,1,0,2:T(8,128)} fusion(bf16[2,32,1,128,256]{4,3,2,1,0:T(8,128)(2,1)} %param.2, bf16[2,4,2,128,128]{4,3,2,1,0:T(8,128)(2,1)} %param.3), kind=kOutput, calls=%fused_computation.21 | convolution fusion | flops 536870912 | bytes 12648448 | tf_op jit(solution)/shard_map/ska,shgac->shgkc/dot_general | solution.py:20
  13.9 0.0 copy-done
  13.9 0.0 copy-done.1
  13.9 5.0 %fusion.16 = f32[2,32,1,128,256]{3,4,1,0,2:T(8,128)} fusion(bf16[2,32,1,128,256]{4,3,2,1,0:T(8,128)(2,1)S(1)} %copy-done, bf16[2,4,2,128,128]{4,3,2,1,0:T(8,128)(2,1)S(1)} %copy-done.1), kind=kOutput, calls=%fused_computation.20 | convolution fusion | flops 536870912 | bytes 12648448 | tf_op jit(solution)/shard_map/ska,shgac->shgkc/dot_general | solution.py:17
  18.9 0.1 copy.72
  19.1 6.8 %fusion.28 = (bf16[2,32,128,128]{2,3,1,0:T(8,128)(2,1)S(1)}, bf16[2,32,128,128]{2,3,1,0:T(8,128)(2,1)S(1)}) fusion(f32[2,32,1,128,256]{3,4,1,0,2:T(8,128)} %fusion.19, f32[2,32,1,128,256]{3,4,1,0,2:T(8,128)} %fusion.16), kind=kLoop, calls=%fused_computation.26 | loop fusion | flops 4194304 | bytes 20971520 | tf_op jit(solution)/shard_map/concatenate | solution.py:25
  25.9 2.0 fusion.22
  27.9 2.4 %copy.47 = bf16[2,32,1,8,16,256]{5,4,1,0,2,3:T(8,128)(2,1)} copy(bf16[2,32,1,8,16,256]{5,4,3,1,0,2:T(8,128)(2,1)S(1)} %bitcast.113) | data formatting | bytes 8388608 | tf_op jit(solution)/shard_map/reshape | solution.py:39
  30.3 5.2 %all-to-all-start = ((bf16[2,32,1,8,16,256]{5,4,1,0,2,3:T(8,128)(2,1)}), bf16[2,32,1,8,16,256]{5,4,1,0,2,3:T(8,128)(2,1)}, u32[]{:S(2)}, u32[]{:S(2)}) async-start(bf16[2,32,1,8,16,256]{5,4,1,0,2,3:T(8,128)(2,1)} %copy.47), calls=%async_computation | async-start | bytes 8388608 | tf_op jit(solution)/shard_map/all_to_all | solution.py:41
  35.4 0.2 reduce-scatter.2.cloned.1.call-start
  35.6 0.1 copy.75
  35.8 48.8 %all-to-all-done = bf16[2,32,1,8,16,256]{5,4,1,0,2,3:T(8,128)(2,1)} async-done(((bf16[2,32,1,8,16,256]{5,4,1,0,2,3:T(8,128)(2,1)}), bf16[2,32,1,8,16,256]{5,4,1,0,2,3:T(8,128)(2,1)}, u32[]{:S(2)}, u32[]{:S(2)}) %all-to-all-start) | async-done | bytes 4194336 | tf_op jit(solution)/shard_map/all_to_all | solution.py:41
  84.6 2.8 %copy.48 = bf16[2,32,1,8,16,256]{5,4,3,1,0,2:T(8,128)(2,1)S(1)} copy(bf16[2,32,1,8,16,256]{5,4,1,0,2,3:T(8,128)(2,1)} %all-to-all-done) | data formatting | bytes 8388608 | tf_op jit(solution)/shard_map/all_to_all | solution.py:41
  87.4 1.8 convolution_bitcast_fusion
  89.2 1.8 convolution_bitcast_fusion.1
  91.0 1.8 fusion.30
  92.8 3.3 %fusion.25 = f32[32,128,256]{2,1,0:T(8,128)} fusion(bf16[2,32,128,128]{2,3,1,0:T(8,128)(2,1)S(1)} %get-tuple-element.6, bf16[2,32,128,128]{2,3,1,0:T(8,128)(2,1)S(1)} %get-tuple-element.5, bf16[2,128,128]{2,1,0:T(8,128)(2,1)S(1)} %get-tuple-element.12, bf16[2,128,128]{2,1,0:T(8,128)(2,1)S(1)} %fusion.55, bf16[2,128,128]{2,1,0:T(8,128)(2,1)S(1)} %get-tuple-element.11), kind=kOutput, calls=%fused_computation.25 | convolution fusion | flops 1083179008 | bytes 8585216 | tf_op jit(solution)/shard_map/shgac,scd->shgad/dot_general | solution.py:29
  96.1 0.0 reduce-scatter.2.cloned.1.call-update
  96.1 77.1 %reduce-scatter.2.cloned.1.call-done = f32[8,128,256]{2,1,0:T(8,128)} async-done(((f32[32,128,256]{2,1,0:T(8,128)}), f32[8,128,256]{2,1,0:T(8,128)}) %reduce-scatter.2.cloned.1.call-update) | async-done | bytes 1048592 | tf_op jit(solution)/shard_map/reduce_scatter | solution.py:47
  173.2 1.3 copy.55
  174.5 18.8 %all_to_all.8 = f32[8,8,1,16,256]{4,3,0,2,1:T(8,128)S(1)} all-to-all(f32[8,8,1,16,256]{4,3,0,2,1:T(8,128)S(1)} %copy.55), channel_id=1, replica_groups=mesh['cuts'=4,'amp'=8] {'amp'}, dimensions={1} | all-to-all | bytes 2097152 | tf_op jit(solution)/shard_map/all_to_all | solution.py:50
  193.3 1.1 copy.56
  (5 shorter events, 0.1 us)
Async XLA Ops:
  6.5 7.3 %copy-start = (bf16[2,32,1,128,256]{4,3,2,1,0:T(8,128)(2,1)S(1)}, bf16[2,32,1,128,256]{4,3,2,1,0:T(8,128)(2,1)}, u32[]{:S(2)}) copy-start(bf16[2,32,1,128,256]{4,3,2,1,0:T(8,128)(2,1)} %param.2) | copy-start | bytes 12582916
  6.5 7.3 %copy-start.1 = (bf16[2,4,2,128,128]{4,3,2,1,0:T(8,128)(2,1)S(1)}, bf16[2,4,2,128,128]{4,3,2,1,0:T(8,128)(2,1)}, u32[]{:S(2)}) copy-start(bf16[2,4,2,128,128]{4,3,2,1,0:T(8,128)(2,1)} %param.3) | copy-start | bytes 1572868
  30.3 54.4 %all-to-all-start = ((bf16[2,32,1,8,16,256]{5,4,1,0,2,3:T(8,128)(2,1)}), bf16[2,32,1,8,16,256]{5,4,1,0,2,3:T(8,128)(2,1)}, u32[]{:S(2)}, u32[]{:S(2)}) async-start(bf16[2,32,1,8,16,256]{5,4,1,0,2,3:T(8,128)(2,1)} %copy.47), calls=%async_computation | async-start | bytes 8388608 | tf_op jit(solution)/shard_map/all_to_all | solution.py:41
  35.4 137.8 %reduce-scatter.2.cloned.1.call-start = ((), (), s32[]{:S(2)}) async-start(), calls=%async_computation.3 | async-start | bytes 5242880 | tf_op jit(solution)/shard_map/reduce_scatter | solution.py:47
Sparse Core Ops, SparseCore 0:
  96.2 76.8 reduce-scatter.1
where the time goes:
time: 202 us; the launch traced here: 201 us
  waiting for transfers between devices  126 us (62%)
  matrix products  21.1 us (10%)
  blocking collectives  18.8 us (9%)
  between operations  13.5 us (7%)
  other arithmetic  8.68 us (4%)
  local copies, waits for them, and re-layouts  7.85 us (4%)
  starting transfers between devices  5.39 us (3%)
    reduce_scatter x1, waiting for transfers between devices, per_device(): summed = lax.psum_scatter(total, 'cuts', scatter_dimension=0, tiled=True)  77.1 us
    all_to_all x1, waiting for transfers between devices, per_device(): lax.all_to_all(split_state, 'amp', split_axis=3, concat_axis=2, tiled=True)  48.8 us
    all_to_all x1, blocking collectives, per_device(): lax.all_to_all(outgoing, 'amp', split_axis=1, concat_axis=2, tiled=True)  18.8 us
    dot_general x2, matrix products, on_rows(): jnp.einsum('ska,shgac->shgkc', imag_gates, values, preferred_element_type...  9.1 us
    concatenate x2, other arithmetic, on_rows(): return jnp.concatenate([real_out, imag_out], axis=-1)  8.65 us
    dot_general x2, matrix products, on_rows(): jnp.einsum('ska,shgac->shgkc', real_gates, values, preferred_element_type...  6.77 us
    dot_general x2, matrix products, on_last(): jnp.einsum('shgac,scd->shgad', values, matrices, preferred_element_type=j...  5.22 us
    all_to_all x1, starting transfers between devices, per_device(): lax.all_to_all(split_state, 'amp', split_axis=3, concat_axis=2, tiled=True)  5.17 us
  transfers between devices with their start and end apart: 2, of which 2 were waited for; matrix products, arithmetic and copies ran while one was open for 0% of the time, Pallas kernels for 0%

commit v1 on v0

--- a/solution.py
+++ b/solution.py
@@ -1,7 +1,14 @@
+import functools
+
 import jax
 import jax.numpy as jnp
 from jax import lax
+from jax.experimental import pallas as pl
+from jax.experimental.pallas import tpu as pltpu
 from jax.sharding import PartitionSpec as P
+
+MESH = pl.DeviceIdType.MESH
+WINDOW = 2
 
 
 def block_matrix(gate):
@@ -29,7 +36,7 @@
     return jnp.einsum("shgac,scd->shgad", values, matrices, preferred_element_type=jnp.float32)
 
 
-def per_device(stem_state, gates):
+def per_device_general(stem_state, gates):
     groups = lax.axis_size("amp")
     slice_count, hidden, single, width, columns = stem_state.shape
     low = width // groups
@@ -51,6 +58,261 @@
     return owned.reshape(share, 1, width, columns)
 
 
+def dot(a, b):
+    return jnp.dot(a, b, preferred_element_type=jnp.float32)
+
+
+def pair_of(first, second):
+    half = first.shape[1] // 2
+    return jnp.concatenate(
+        [
+            jnp.concatenate([first[:, :half], second[:, :half]], axis=1),
+            jnp.concatenate([first[:, half:], second[:, half:]], axis=1),
+        ],
+        axis=0,
+    )
+
+
+def kernel(cuts, groups, stem, gates, out, land, gate_buf, blocks, moved, parts, arrived, own,
+           stage, in_send, in_recv, z_send, z_recv, back_send, back_recv, local_sem, gate_sem,
+           own_sem):
+    slices = stem.shape[0]
+    width = stem.shape[3]
+    columns = stem.shape[4]
+    low = width // groups
+    k = lax.axis_index("cuts")
+    j = lax.axis_index("amp")
+
+    barrier = pltpu.get_barrier_semaphore()
+    for i in range(1, groups):
+        pl.semaphore_signal(barrier, inc=1, device_id=(k, lax.rem(j + i, groups)), device_id_type=MESH)
+    for i in range(1, cuts):
+        pl.semaphore_signal(barrier, inc=1, device_id=(lax.rem(k + i, cuts), j), device_id_type=MESH)
+    gate_copy = pltpu.make_async_copy(gates, gate_buf, gate_sem)
+    gate_copy.start()
+
+    half = k // 2
+    order = [3 * (1 - half), 2 - half, 4 * half + 1 - k, k]
+
+    def local_in(step):
+        return pltpu.make_async_copy(
+            stem.at[:, order[step] * groups + j, 0], land.at[step, :, j], local_sem.at[step]
+        )
+
+    def send_in(step, i):
+        peer = lax.rem(j + i, groups)
+        return pltpu.make_async_remote_copy(
+            src_ref=stem.at[:, order[step] * groups + peer, 0],
+            dst_ref=land.at[step, :, j],
+            send_sem=in_send.at[step, i - 1],
+            recv_sem=in_recv.at[step, i - 1],
+            device_id=(k, peer),
+            device_id_type=MESH,
+        )
+
+    def arrive_in(step, i):
+        peer = lax.rem(j + groups - i, groups)
+        return pltpu.make_async_remote_copy(
+            src_ref=land.at[step, :, peer],
+            dst_ref=land.at[step, :, peer],
+            send_sem=in_send.at[step, i - 1],
+            recv_sem=in_recv.at[step, i - 1],
+            device_id=(k, peer),
+            device_id_type=MESH,
+        )
+
+    def issue(step):
+        for i in range(1, groups):
+            send_in(step, i).start()
+
+    for step in range(cuts):
+        local_in(step).start()
+    pl.semaphore_wait(barrier, groups - 1 + cuts - 1)
+    for step in range(WINDOW):
+        issue(step)
+
+    gate_copy.wait()
+    for s in range(slices):
+        for n in range(4):
+            re = gate_buf[s, n, 0]
+            im = gate_buf[s, n, 1]
+            if n % 2 == 0:
+                blocks[s, n, :width, :width] = re
+                blocks[s, n, :width, width:] = -im
+                blocks[s, n, width:, :width] = im
+                blocks[s, n, width:, width:] = re
+            else:
+                re = re.T
+                im = im.T
+                blocks[s, n, :width, :width] = re
+                blocks[s, n, :width, width:] = im
+                blocks[s, n, width:, :width] = -im
+                blocks[s, n, width:, width:] = re
+
+    def rows_then_last(pair, s, n):
+        mid = dot(blocks[s, n], pair).astype(jnp.bfloat16)
+        turned = jnp.concatenate(
+            [
+                jnp.concatenate([mid[:width, :width], mid[width:, :width]], axis=1),
+                jnp.concatenate([mid[:width, width:], mid[width:, width:]], axis=1),
+            ],
+            axis=0,
+        )
+        return dot(turned, blocks[s, n + 1])
+
+    def compute(step, write):
+        for s in range(slices):
+            @pl.loop(0, groups // 2)
+            def _(m, s=s):
+                g = 2 * m
+                res = rows_then_last(
+                    pair_of(land[step, s, g], land[step, s, g + 1]), s, 0
+                ).astype(jnp.bfloat16)
+                for d in range(2):
+                    for p in range(groups):
+                        moved[s, p, pl.ds(pl.multiple_of((g + d) * low, low), low), :] = (
+                            res[d * width + p * low : d * width + (p + 1) * low]
+                        )
+
+        @pl.loop(0, groups // 2)
+        def _(m):
+            p = 2 * m
+            total = None
+            for s in range(slices):
+                term = rows_then_last(pair_of(moved[s, p], moved[s, p + 1]), s, 2)
+                total = term if total is None else total + term
+            for d in range(2):
+                for g in range(groups):
+                    write(g, p + d, total[d * width + g * low : d * width + (g + 1) * low])
+
+    def z_copy(step):
+        slot = lax.rem(k - order[step] + cuts - 1, cuts)
+        return pltpu.make_async_remote_copy(
+            src_ref=parts.at[step],
+            dst_ref=arrived.at[slot],
+            send_sem=z_send.at[step],
+            recv_sem=z_recv.at[slot],
+            device_id=(order[step], j),
+            device_id_type=MESH,
+        )
+
+    for step in range(cuts):
+        local_in(step).wait()
+        for i in range(1, groups):
+            arrive_in(step, i).wait_recv()
+        if step + WINDOW < cuts:
+            for i in range(1, groups):
+                send_in(step, i).wait_send()
+            issue(step + WINDOW)
+        if step < cuts - 1:
+            def write(g, p, rows, step=step):
+                parts[step, g, pl.ds(pl.multiple_of(p * low, low), low), :] = rows.astype(jnp.bfloat16)
+        else:
+            def write(g, p, rows):
+                own[g, pl.ds(pl.multiple_of(p * low, low), low), :] = rows
+        compute(step, write)
+        if step < cuts - 1:
+            z_copy(step).start()
+
+    for slot in range(cuts - 1):
+        pltpu.make_async_remote_copy(
+            src_ref=arrived.at[slot],
+            dst_ref=arrived.at[slot],
+            send_sem=z_send.at[slot],
+            recv_sem=z_recv.at[slot],
+            device_id=(lax.rem(k + slot + 1, cuts), j),
+            device_id_type=MESH,
+        ).wait_recv()
+
+    def back(i):
+        peer = lax.rem(j + i, groups)
+        return pltpu.make_async_remote_copy(
+            src_ref=stage.at[peer],
+            dst_ref=out.at[j],
+            send_sem=back_send.at[i - 1],
+            recv_sem=back_recv.at[i - 1],
+            device_id=(k, peer),
+            device_id_type=MESH,
+        )
+
+    own_copy = pltpu.make_async_copy(stage.at[j], out.at[j], own_sem)
+    for i in list(range(1, groups)) + [0]:
+        peer = lax.rem(j + i, groups)
+        total = own[peer]
+        for slot in range(cuts - 1):
+            total = total + arrived[slot, peer].astype(jnp.float32)
+        stage[peer] = total.astype(jnp.bfloat16)
+        if i > 0:
+            back(i).start()
+        else:
+            own_copy.start()
+
+    for step in range(max(cuts - WINDOW, 0), cuts):
+        for i in range(1, groups):
+            send_in(step, i).wait_send()
+    for step in range(cuts - 1):
+        z_copy(step).wait_send()
+    for i in range(1, groups):
+        back(i).wait_send()
+    for i in range(1, groups):
+        peer = lax.rem(j + groups - i, groups)
+        pltpu.make_async_remote_copy(
+            src_ref=stage.at[peer],
+            dst_ref=out.at[peer],
+            send_sem=back_send.at[i - 1],
+            recv_sem=back_recv.at[i - 1],
+            device_id=(k, peer),
+            device_id_type=MESH,
+        ).wait_recv()
+    own_copy.wait()
+
+
+def per_device_fused(stem_state, gates):
+    cuts = lax.axis_size("cuts")
+    groups = lax.axis_size("amp")
+    slices, hidden, single, width, columns = stem_state.shape
+    state = (groups, width, columns)
+    bf16 = jnp.bfloat16
+    result = pl.pallas_call(
+        functools.partial(kernel, cuts, groups),
+        out_shape=jax.ShapeDtypeStruct(state, bf16),
+        in_specs=[pl.BlockSpec(memory_space=pl.ANY)] * 2,
+        out_specs=pl.BlockSpec(memory_space=pl.ANY),
+        scratch_shapes=[
+            pltpu.VMEM((cuts, slices) + state, bf16),
+            pltpu.VMEM(gates.shape, bf16),
+            pltpu.VMEM((slices, 4, columns, columns), bf16),
+            pltpu.VMEM((slices,) + state, bf16),
+            pltpu.VMEM((cuts - 1,) + state, bf16),
+            pltpu.VMEM((cuts - 1,) + state, bf16),
+            pltpu.VMEM(state, jnp.float32),
+            pltpu.VMEM(state, bf16),
+            pltpu.SemaphoreType.DMA((cuts, groups - 1)),
+            pltpu.SemaphoreType.DMA((cuts, groups - 1)),
+            pltpu.SemaphoreType.DMA((cuts - 1,)),
+            pltpu.SemaphoreType.DMA((cuts - 1,)),
+            pltpu.SemaphoreType.DMA((groups - 1,)),
+            pltpu.SemaphoreType.DMA((groups - 1,)),
+            pltpu.SemaphoreType.DMA((cuts,)),
+            pltpu.SemaphoreType.DMA,
+            pltpu.SemaphoreType.DMA,
+        ],
+        compiler_params=pltpu.CompilerParams(
+            collective_id=0, has_side_effects=True, vmem_limit_bytes=40 * 1024 * 1024
+        ),
+    )(stem_state, gates)
+    return result.astype(jnp.float32).reshape(hidden // cuts, 1, width, columns)
+
+
+def per_device(stem_state, gates):
+    cuts = lax.axis_size("cuts")
+    groups = lax.axis_size("amp")
+    hidden, width = stem_state.shape[1], stem_state.shape[3]
+    if cuts == 4 and hidden == cuts * groups and width % (16 * groups) == 0 and groups % 2 == 0:
+        return per_device_fused(stem_state, gates)
+    return per_device_general(stem_state, gates)
+
+
 def solution(mesh):
     placed = (P("cuts", None, "amp", None, None), P("cuts", None, None, None, None))
     return jax.shard_map(

time: 202 us -> 80.6 us (0.40)
  waiting for transfers between devices: 126 us -> 0 us
  Pallas kernels: 0 us -> 74.8 us
  matrix products: 21.1 us -> 0 us
  blocking collectives: 18.8 us -> 0 us
  between operations: 13.5 us -> 0.01 us
  other arithmetic: 8.68 us -> 1.06 us
  starting transfers between devices: 5.39 us -> 0 us
  local copies, waits for them, and re-layouts: 7.85 us -> 3.23 us
    reduce_scatter x1 -> x0, waiting for transfers between devices: 77.1 us -> none  [per_device(): summed = lax.psum_scatter(total, 'cuts', scatter_dimension=0, tiled=True)]
    pallas_call x0 -> x1, Pallas kernels: none -> 74.8 us  [per_device_fused(): pl.pallas_call(functools.partial(kernel, cuts, groups), out_shape=jax.Sha...]
    all_to_all x1 -> x0, waiting for transfers between devices: 48.8 us -> none  [per_device(): lax.all_to_all(split_state, 'amp', split_axis=3, concat_axis=2, tiled=True)]
    dot_general x6 -> x0, matrix products: 21.1 us -> none  [the longest x2 9.1 us: on_rows(): jnp.einsum('ska,shgac->shgkc', imag_gates, values, preferred_element_type...]
    all_to_all x1 -> x0, blocking collectives: 18.8 us -> none  [per_device(): lax.all_to_all(outgoing, 'amp', split_axis=1, concat_axis=2, tiled=True)]
    concatenate x2 -> x0, other arithmetic: 8.65 us -> none  [on_rows(): return jnp.concatenate([real_out, imag_out], axis=-1)]
    all_to_all x1 -> x0, starting transfers between devices: 5.17 us -> none  [per_device(): lax.all_to_all(split_state, 'amp', split_axis=3, concat_axis=2, tiled=True)]
    all_to_all x2 -> x0, local copies, waits for them, and re-layouts: 3.85 us -> none  [the longest x1 2.79 us: per_device(): lax.all_to_all(split_state, 'amp', split_axis=3, concat_axis=2, tiled=True)]
  transfers between devices with their start and end apart: 2 -> 0, of which waited for: 2 -> 0; matrix products, arithmetic and copies ran while one was open for 0% -> 0% of each run, Pallas kernels for 0% -> 0%
where the time goes in v1:
time: 80.6 us; the launch traced here: 79.1 us
  Pallas kernels  74.8 us (93%)
  local copies, waits for them, and re-layouts  3.23 us (4%)
  other arithmetic  1.06 us (1%)
    pallas_call x1, Pallas kernels, per_device_fused(): pl.pallas_call(functools.partial(kernel, cuts, groups), out_shape=jax.Sha...  74.8 us
    unnamed x4, local copies, waits for them, and re-layouts  3.23 us

profile of v1, /device:TPU:0, one launch (start us, length us, event | category | flops | bytes accessed | tf_op | source)
XLA Modules:
  0.0 79.1 jit_solution(11921769879995685301)
XLA Ops:
  0.0 0.0 copy-start
  0.0 2.2 %copy-done = bf16[2,32,1,128,256]{4,3,2,1,0:T(8,128)(2,1)S(1)} copy-done((bf16[2,32,1,128,256]{4,3,2,1,0:T(8,128)(2,1)S(1)}, bf16[2,32,1,128,256]{4,3,2,1,0:T(8,128)(2,1)}, u32[]{:S(2)}) %copy-start) | copy-done | bytes 4194328
  2.2 0.0 copy-start.1
  2.2 1.0 %copy-done.1 = bf16[2,4,2,128,128]{4,3,2,1,0:T(8,128)(2,1)S(1)} copy-done((bf16[2,4,2,128,128]{4,3,2,1,0:T(8,128)(2,1)S(1)}, bf16[2,4,2,128,128]{4,3,2,1,0:T(8,128)(2,1)}, u32[]{:S(2)}) %copy-start.1) | copy-done | bytes 524312
  3.2 74.8 %shard_map.28 = bf16[8,128,256]{2,1,0:T(8,128)(2,1)S(1)} custom-call(bf16[2,32,1,128,256]{4,3,2,1,0:T(8,128)(2,1)S(1)} %copy-done, bf16[2,4,2,128,128]{4,3,2,1,0:T(8,128)(2,1)S(1)} %copy-done.1), custom_call_target="tpu_custom_call" | custom-call | tf_op jit(solution)/shard_map/pallas_call | solution.py:276
  78.1 1.1 %bitcast_convert_fusion = f32[8,1,128,256]{3,2,1,0:T(8,128)} fusion(bf16[8,128,256]{2,1,0:T(8,128)(2,1)S(1)} %shard_map.28), kind=kLoop, calls=%fused_computation | loop fusion | flops 262144 | bytes 1572864 | tf_op jit(solution)/shard_map/reshape | solution.py:304
Async XLA Ops:
  0.0 2.2 %copy-start = (bf16[2,32,1,128,256]{4,3,2,1,0:T(8,128)(2,1)S(1)}, bf16[2,32,1,128,256]{4,3,2,1,0:T(8,128)(2,1)}, u32[]{:S(2)}) copy-start(bf16[2,32,1,128,256]{4,3,2,1,0:T(8,128)(2,1)} %stem.1) | copy-start | bytes 12582916
  2.2 1.0 %copy-start.1 = (bf16[2,4,2,128,128]{4,3,2,1,0:T(8,128)(2,1)S(1)}, bf16[2,4,2,128,128]{4,3,2,1,0:T(8,128)(2,1)}, u32[]{:S(2)}) copy-start(bf16[2,4,2,128,128]{4,3,2,1,0:T(8,128)(2,1)} %gates.1) | copy-start | bytes 1572868

commit v2 on v1

v2 whole, which is shorter than its diff:
```python
import functools

import jax
import jax.numpy as jnp
from jax import lax
from jax.experimental import pallas as pl
from jax.experimental.pallas import tpu as pltpu
from jax.sharding import PartitionSpec as P

MESH = pl.DeviceIdType.MESH


def block_matrix(gate):
    real_part = gate[0]
    imag_part = gate[1]
    top = jnp.concatenate([real_part.T, imag_part.T], axis=1)
    bottom = jnp.concatenate([-imag_part.T, real_part.T], axis=1)
    return jnp.concatenate([top, bottom], axis=0)


def on_rows(values, real_gates, imag_gates):
    width = values.shape[-1] // 2
    first_term = jnp.einsum(
        "ska,shgac->shgkc", real_gates, values, preferred_element_type=jnp.float32
    )
    second_term = jnp.einsum(
        "ska,shgac->shgkc", imag_gates, values, preferred_element_type=jnp.float32
    )
    real_out = first_term[..., :width] - second_term[..., width:]
    imag_out = first_term[..., width:] + second_term[..., :width]
    return jnp.concatenate([real_out, imag_out], axis=-1)


def on_last(values, matrices):
    return jnp.einsum("shgac,scd->shgad", values, matrices, preferred_element_type=jnp.float32)


def per_device_general(stem_state, gates):
    groups = lax.axis_size("amp")
    slice_count, hidden, single, width, columns = stem_state.shape
    low = width // groups
    first = on_rows(stem_state, gates[:, 0, 0], gates[:, 0, 1]).astype(jnp.bfloat16)
    second_matrix = jax.vmap(block_matrix)(gates[:, 1])
    second = on_last(first, second_matrix).astype(jnp.bfloat16)
    split_state = second.reshape(slice_count, hidden, 1, groups, low, columns)
    last_matrix = jax.vmap(block_matrix)(gates[:, 3])
    pieces = lax.all_to_all(split_state, "amp", split_axis=3, concat_axis=2, tiled=True)
    count = pieces.shape[1]
    merged = pieces.reshape(slice_count, count, 1, width, columns)
    third = on_rows(merged, gates[:, 2, 0], gates[:, 2, 1]).astype(jnp.bfloat16)
    fourth = on_last(third, last_matrix).reshape(slice_count, count, width, columns)
    total = jnp.sum(fourth, axis=0)
    summed = lax.psum_scatter(total, "cuts", scatter_dimension=0, tiled=True)
    share = summed.shape[0]
    outgoing = summed.reshape(share, groups, 1, low, columns)
    owned = lax.all_to_all(outgoing, "amp", split_axis=1, concat_axis=2, tiled=True)
    return owned.reshape(share, 1, width, columns)


def dot(a, b):
    return jnp.dot(a, b, preferred_element_type=jnp.float32)


def pair_of(first, second):
    half = first.shape[1] // 2
    return jnp.concatenate(
        [
            jnp.concatenate([first[:, :half], second[:, :half]], axis=1),
            jnp.concatenate([first[:, half:], second[:, half:]], axis=1),
        ],
        axis=0,
    )


def kernel(cuts, groups, stem, gates, out, land, gate_buf, blocks, moved, parts, slots, own,
           stage, in_send, in_recv, z_send, z_recv, back_send, back_recv, local_sem, gate_sem,
           own_sem):
    slices = stem.shape[0]
    width = stem.shape[3]
    low = width // groups
    k = lax.axis_index("cuts")
    j = lax.axis_index("amp")

    barrier = pltpu.get_barrier_semaphore()
    for i in range(1, groups):
        pl.semaphore_signal(barrier, inc=1, device_id=(k, lax.rem(j + i, groups)), device_id_type=MESH)
    for i in range(1, cuts):
        pl.semaphore_signal(barrier, inc=1, device_id=(lax.rem(k + i, cuts), j), device_id_type=MESH)
    gate_copy = pltpu.make_async_copy(gates, gate_buf, gate_sem)
    gate_copy.start()

    half = k // 2
    inner = (k * (3 - k)) // 2
    outer = 1 - inner
    order = [3 * (1 - half), 2 - half, 4 * half + 1 - k, k]

    def local_in(step, s):
        return pltpu.make_async_copy(
            stem.at[s, order[step] * groups + j, 0], land.at[step, s, j], local_sem.at[step, s]
        )

    def send_in(step, s, i):
        peer = lax.rem(j + i, groups)
        return pltpu.make_async_remote_copy(
            src_ref=stem.at[s, order[step] * groups + peer, 0],
            dst_ref=land.at[step, s, j],
            send_sem=in_send.at[step, s, i - 1],
            recv_sem=in_recv.at[step, s, i - 1],
            device_id=(k, peer),
            device_id_type=MESH,
        )

    def arrive_in(step, s, i):
        peer = lax.rem(j + groups - i, groups)
        return pltpu.make_async_remote_copy(
            src_ref=land.at[step, s, peer],
            dst_ref=land.at[step, s, peer],
            send_sem=in_send.at[step, s, i - 1],
            recv_sem=in_recv.at[step, s, i - 1],
            device_id=(k, peer),
            device_id_type=MESH,
        )

    pl.semaphore_wait(barrier, groups - 1 + cuts - 1)
    for step in range(cuts):
        for s in range(slices):
            for i in range(1, groups):
                send_in(step, s, i).start()
            local_in(step, s).start()

    gate_copy.wait()
    for s in range(slices):
        for n in range(4):
            re = gate_buf[s, n, 0]
            im = gate_buf[s, n, 1]
            if n % 2 == 0:
                blocks[s, n, :width, :width] = re
                blocks[s, n, :width, width:] = -im
                blocks[s, n, width:, :width] = im
                blocks[s, n, width:, width:] = re
            else:
                re = re.T
                im = im.T
                blocks[s, n, :width, :width] = re
                blocks[s, n, :width, width:] = im
                blocks[s, n, width:, :width] = -im
                blocks[s, n, width:, width:] = re

    def rows_then_last(pair, s, n):
        mid = dot(blocks[s, n], pair).astype(jnp.bfloat16)
        turned = jnp.concatenate(
            [
                jnp.concatenate([mid[:width, :width], mid[width:, :width]], axis=1),
                jnp.concatenate([mid[:width, width:], mid[width:, width:]], axis=1),
            ],
            axis=0,
        )
        return dot(turned, blocks[s, n + 1])

    def first_two(step, s):
        @pl.loop(0, groups // 2)
        def _(m):
            g = 2 * m
            res = rows_then_last(
                pair_of(land[step, s, g], land[step, s, g + 1]), s, 0
            ).astype(jnp.bfloat16)
            for d in range(2):
                for p in range(groups):
                    moved[p, pl.ds(pl.multiple_of((g + d) * low, low), low), :] = (
                        res[d * width + p * low : d * width + (p + 1) * low]
                    )

    def last_two(s, start, stop, write):
        @pl.loop(start, stop)
        def _(m):
            p = 2 * m
            total = rows_then_last(pair_of(moved[p], moved[p + 1]), s, 2)
            for d in range(2):
                rows = total[d * width : (d + 1) * width]
                if s > 0:
                    rows = own[p + d] + rows
                if s < slices - 1:
                    own[p + d] = rows
                else:
                    for g in range(groups):
                        write(g, p + d, rows[g * low : (g + 1) * low])

    def z_copy(step):
        if step < 2:
            slot = step * outer + 2 * inner
            target = outer * (1 + half) + inner * order[step]
        else:
            slot = 3
            target = order[step]
        return pltpu.make_async_remote_copy(
            src_ref=parts.at[step],
            dst_ref=slots.at[slot],
            send_sem=z_send.at[step],
            recv_sem=z_recv.at[slot],
            device_id=(target, j),
            device_id_type=MESH,
        )

    def wait_slot(slot):
        pltpu.make_async_remote_copy(
            src_ref=slots.at[slot],
            dst_ref=slots.at[slot],
            send_sem=z_send.at[0],
            recv_sem=z_recv.at[slot],
            device_id=(lax.rem(k + 1, cuts), j),
            device_id_type=MESH,
        ).wait_recv()

    def merge(step):
        @pl.when(inner == 1)
        def _():
            wait_slot(step)
            @pl.loop(0, groups)
            def _(g):
                both = parts[step, g].astype(jnp.float32) + slots[step, g].astype(jnp.float32)
                parts[step, g] = both.astype(jnp.bfloat16)
            z_copy(step).start()

    def back(i, part):
        peer = lax.rem(j + i, groups)
        rows = pl.ds(part * (width // 2), width // 2)
        return pltpu.make_async_remote_copy(
            src_ref=stage.at[peer, rows],
            dst_ref=out.at[j, rows],
            send_sem=back_send.at[part, i - 1],
            recv_sem=back_recv.at[part, i - 1],
            device_id=(k, peer),
            device_id_type=MESH,
        )

    def arrive_back(i, part):
        peer = lax.rem(j + groups - i, groups)
        rows = pl.ds(part * (width // 2), width // 2)
        return pltpu.make_async_remote_copy(
            src_ref=stage.at[peer, rows],
            dst_ref=out.at[peer, rows],
            send_sem=back_send.at[part, i - 1],
            recv_sem=back_recv.at[part, i - 1],
            device_id=(k, peer),
            device_id_type=MESH,
        )

    for step in range(cuts):
        def write(g, p, rows, step=step):
            parts[step, g, pl.ds(pl.multiple_of(p * low, low), low), :] = rows.astype(jnp.bfloat16)

        def write_last(g, p, rows):
            at = pl.ds(pl.multiple_of(p * low, low), low)
            for slot in (2, 3):
                rows = rows + slots[slot, g, at, :].astype(jnp.float32)
            stage[g, at, :] = rows.astype(jnp.bfloat16)

        for s in range(slices):
            local_in(step, s).wait()
            for i in range(1, groups):
                arrive_in(step, s, i).wait_recv()
            first_two(step, s)
            if step < cuts - 1 or s < slices - 1:
                last_two(s, 0, groups // 2, write)
            else:
                wait_slot(2)
                wait_slot(3)
                for part in range(2):
                    last_two(s, part * groups // 4, (part + 1) * groups // 4, write_last)
                    for i in range(1, groups):
                        back(i, part).start()
        if step == 2:
            z_copy(step).start()
        if step < 2:
            @pl.when(outer == 1)
            def _(step=step):
                z_copy(step).start()
        if step in (1, 2):
            merge(step - 1)

    own_copy = pltpu.make_async_copy(stage.at[j], out.at[j], own_sem)
    own_copy.start()
    for step in range(cuts):
        for s in range(slices):
            for i in range(1, groups):
                send_in(step, s, i).wait_send()
    for step in range(cuts - 1):
        z_copy(step).wait_send()
    for part in range(2):
        for i in range(1, groups):
            back(i, part).wait_send()
    for part in range(2):
        for i in range(1, groups):
            arrive_back(i, part).wait_recv()
    own_copy.wait()


def per_device_fused(stem_state, gates):
    cuts = lax.axis_size("cuts")
    groups = lax.axis_size("amp")
    slices, hidden, single, width, columns = stem_state.shape
    state = (groups, width, columns)
    bf16 = jnp.bfloat16
    result = pl.pallas_call(
        functools.partial(kernel, cuts, groups),
        out_shape=jax.ShapeDtypeStruct(state, bf16),
        in_specs=[pl.BlockSpec(memory_space=pltpu.HBM)] * 2,
        out_specs=pl.BlockSpec(memory_space=pl.ANY),
        scratch_shapes=[
            pltpu.VMEM((cuts, slices) + state, bf16),
            pltpu.VMEM(gates.shape, bf16),
            pltpu.VMEM((slices, 4, columns, columns), bf16),
            pltpu.VMEM(state, bf16),
            pltpu.VMEM((cuts - 1,) + state, bf16),
            pltpu.VMEM((4,) + state, bf16),
            pltpu.VMEM(state, jnp.float32),
            pltpu.VMEM(state, bf16),
            pltpu.SemaphoreType.DMA((cuts, slices, groups - 1)),
            pltpu.SemaphoreType.DMA((cuts, slices, groups - 1)),
            pltpu.SemaphoreType.DMA((cuts - 1,)),
            pltpu.SemaphoreType.DMA((4,)),
            pltpu.SemaphoreType.DMA((2, groups - 1)),
            pltpu.SemaphoreType.DMA((2, groups - 1)),
            pltpu.SemaphoreType.DMA((cuts, slices)),
            pltpu.SemaphoreType.DMA,
            pltpu.SemaphoreType.DMA,
        ],
        compiler_params=pltpu.CompilerParams(
            collective_id=0, has_side_effects=True, vmem_limit_bytes=60 * 1024 * 1024
        ),
    )(stem_state, gates)
    return result.astype(jnp.float32).reshape(hidden // cuts, 1, width, columns)


def per_device(stem_state, gates):
    cuts = lax.axis_size("cuts")
    groups = lax.axis_size("amp")
    hidden, width = stem_state.shape[1], stem_state.shape[3]
    if cuts == 4 and hidden == cuts * groups and width % (16 * groups) == 0 and groups % 4 == 0:
        return per_device_fused(stem_state, gates)
    return per_device_general(stem_state, gates)


def solution(mesh):
    placed = (P("cuts", None, "amp", None, None), P("cuts", None, None, None, None))
    return jax.shard_map(
        per_device,
        mesh=mesh,
        in_specs=placed,
        out_specs=P("cuts", "amp", None, None),
        check_vma=False,
    )
```

time: 80.6 us -> 71.6 us (0.89); the launches traced: 79.1 us -> 71.3 us
  Pallas kernels: 74.8 us -> 69.2 us
  local copies, waits for them, and re-layouts: 3.23 us -> 0 us
  other arithmetic: 1.06 us -> 2.11 us
    pallas_call x1, Pallas kernels: 74.8 us -> 69.2 us  [per_device_fused(): pl.pallas_call(functools.partial(kernel, cuts, groups), out_shape=jax.Sha...]
    unnamed x4 -> x0, local copies, waits for them, and re-layouts: 3.23 us -> none
    reshape x1, other arithmetic: 1.06 us -> 2.11 us  [per_device_fused(): return result.astype(jnp.float32).reshape(hidden // cuts, 1, width, columns)]
where the time goes in v2:
time: 71.6 us; the launch traced here: 71.3 us
  Pallas kernels  69.2 us (97%)
  other arithmetic  2.11 us (3%)
    pallas_call x1, Pallas kernels, per_device_fused(): pl.pallas_call(functools.partial(kernel, cuts, groups), out_shape=jax.Sha...  69.2 us
    reshape x1, other arithmetic, per_device_fused(): return result.astype(jnp.float32).reshape(hidden // cuts, 1, width, columns)  2.11 us

profile of v2, /device:TPU:0, one launch (start us, length us, event | category | flops | bytes accessed | tf_op | source)
XLA Modules:
  0.0 71.3 jit_solution(17691072213378869893)
XLA Ops:
  0.0 69.2 %shard_map.28 = bf16[8,128,256]{2,1,0:T(8,128)(2,1)} custom-call(bf16[2,32,1,128,256]{4,3,2,1,0:T(8,128)(2,1)} %stem.1, bf16[2,4,2,128,128]{4,3,2,1,0:T(8,128)(2,1)} %gates.1), custom_call_target="tpu_custom_call" | custom-call | tf_op jit(solution)/shard_map/pallas_call | solution.py:304
  69.2 2.1 %bitcast_convert_fusion = f32[8,1,128,256]{3,2,1,0:T(8,128)} fusion(bf16[8,128,256]{2,1,0:T(8,128)(2,1)} %shard_map.28), kind=kLoop, calls=%fused_computation | loop fusion | flops 262144 | bytes 1572864 | tf_op jit(solution)/shard_map/reshape | solution.py:332

commit v3 on v0

--- a/solution.py
+++ b/solution.py
@@ -1,7 +1,15 @@
+import functools
+
 import jax
 import jax.numpy as jnp
 from jax import lax
+from jax.experimental import pallas as pl
+from jax.experimental.pallas import tpu as pltpu
 from jax.sharding import PartitionSpec as P
+
+MESH = pl.DeviceIdType.MESH
+BATCH = 4
+LAG = 1
 
 
 def block_matrix(gate):
@@ -29,7 +37,7 @@
     return jnp.einsum("shgac,scd->shgad", values, matrices, preferred_element_type=jnp.float32)
 
 
-def per_device(stem_state, gates):
+def per_device_general(stem_state, gates):
     groups = lax.axis_size("amp")
     slice_count, hidden, single, width, columns = stem_state.shape
     low = width // groups
@@ -51,6 +59,300 @@
     return owned.reshape(share, 1, width, columns)
 
 
+def dot(a, b):
+    return jnp.dot(a, b, preferred_element_type=jnp.float32)
+
+
+def pair_of(first, second):
+    half = first.shape[1] // 2
+    return jnp.concatenate(
+        [
+            jnp.concatenate([first[:, :half], second[:, :half]], axis=1),
+            jnp.concatenate([first[:, half:], second[:, half:]], axis=1),
+        ],
+        axis=0,
+    )
+
+
+def kernel(cuts, groups, stem, gates, out, stem_buf, gate_buf, blocks, second, land, parts, slots,
+           stage, in_send, in_recv, z_send, z_recv, back_send, back_recv, stem_sem, own_sem,
+           gate_sem, done_sem):
+    slices, hidden, single, width, columns = stem.shape
+    low = width // groups
+    share = hidden // cuts
+    subs = share // BATCH
+    k = lax.axis_index("cuts")
+    j = lax.axis_index("amp")
+    mine = pl.ds(pl.multiple_of(j * low, low), low)
+
+    barrier = pltpu.get_barrier_semaphore()
+    for i in range(1, groups):
+        pl.semaphore_signal(barrier, inc=1, device_id=(k, lax.rem(j + i, groups)), device_id_type=MESH)
+    for i in range(1, cuts):
+        pl.semaphore_signal(barrier, inc=1, device_id=(lax.rem(k + i, cuts), j), device_id_type=MESH)
+    gate_copy = pltpu.make_async_copy(gates, gate_buf, gate_sem)
+    gate_copy.start()
+
+    half = k // 2
+    inner = (k * (3 - k)) // 2
+    outer = 1 - inner
+    order = [3 * (1 - half), 2 - half, 4 * half + 1 - k, k]
+    steps = [(t, u) for t in range(cuts) for u in range(subs)]
+
+    def load(n):
+        t, u = steps[n]
+        return pltpu.make_async_copy(
+            stem.at[:, pl.ds(order[t] * share + u * BATCH, BATCH), 0], stem_buf.at[n], stem_sem.at[n]
+        )
+
+    for n in range(len(steps)):
+        load(n).start()
+
+    gate_copy.wait()
+    for s in range(slices):
+        for n in range(4):
+            re = gate_buf[s, n, 0]
+            im = gate_buf[s, n, 1]
+            if n % 2 == 0:
+                blocks[s, n, :width, :width] = re
+                blocks[s, n, :width, width:] = -im
+                blocks[s, n, width:, :width] = im
+                blocks[s, n, width:, width:] = re
+            else:
+                re = re.T
+                im = im.T
+                blocks[s, n, :width, :width] = re
+                blocks[s, n, :width, width:] = im
+                blocks[s, n, width:, :width] = -im
+                blocks[s, n, width:, width:] = re
+
+    def rows_then_last(pair, s, n):
+        mid = dot(blocks[s, n], pair).astype(jnp.bfloat16)
+        turned = jnp.concatenate(
+            [
+                jnp.concatenate([mid[:width, :width], mid[width:, :width]], axis=1),
+                jnp.concatenate([mid[:width, width:], mid[width:, width:]], axis=1),
+            ],
+            axis=0,
+        )
+        return dot(turned, blocks[s, n + 1])
+
+    def rows_of(peer):
+        return pl.ds(pl.multiple_of(peer * low, low), low)
+
+    def send_in(n, i):
+        peer = lax.rem(j + i, groups)
+        return pltpu.make_async_remote_copy(
+            src_ref=second.at[n, :, :, rows_of(peer)],
+            dst_ref=land.at[n, :, :, mine],
+            send_sem=in_send.at[n, i - 1],
+            recv_sem=in_recv.at[n, i - 1],
+            device_id=(k, peer),
+            device_id_type=MESH,
+        )
+
+    def arrive_in(n, i):
+        peer = lax.rem(j + groups - i, groups)
+        return pltpu.make_async_remote_copy(
+            src_ref=land.at[n, :, :, rows_of(peer)],
+            dst_ref=land.at[n, :, :, rows_of(peer)],
+            send_sem=in_send.at[n, i - 1],
+            recv_sem=in_recv.at[n, i - 1],
+            device_id=(k, peer),
+            device_id_type=MESH,
+        )
+
+    def keep(n):
+        return pltpu.make_async_copy(
+            second.at[n, :, :, mine], land.at[n, :, :, mine], own_sem.at[n]
+        )
+
+    for n in range(len(steps)):
+        load(n).wait()
+
+        @pl.loop(0, BATCH // 2)
+        def _(m, n=n):
+            h = 2 * m
+            for s in range(slices):
+                res = rows_then_last(pair_of(stem_buf[n, s, h], stem_buf[n, s, h + 1]), s, 0)
+                res = res.astype(jnp.bfloat16)
+                second[n, s, h] = res[:width]
+                second[n, s, h + 1] = res[width:]
+
+        if n == 0:
+            pl.semaphore_wait(barrier, groups - 1 + cuts - 1)
+        for i in range(1, groups):
+            send_in(n, i).start()
+        keep(n).start()
+
+    def z_copy(t, u):
+        if t < 2:
+            slot = t * outer + 2 * inner
+            target = outer * (1 + half) + inner * order[t]
+        else:
+            slot = 3
+            target = order[t]
+        return pltpu.make_async_remote_copy(
+            src_ref=parts.at[t, u],
+            dst_ref=slots.at[slot, u],
+            send_sem=z_send.at[t, u],
+            recv_sem=z_recv.at[slot, u],
+            device_id=(target, j),
+            device_id_type=MESH,
+        )
+
+    def wait_slot(slot, u):
+        pltpu.make_async_remote_copy(
+            src_ref=slots.at[slot, u],
+            dst_ref=slots.at[slot, u],
+            send_sem=z_send.at[0, u],
+            recv_sem=z_recv.at[slot, u],
+            device_id=(lax.rem(k + 1, cuts), j),
+            device_id_type=MESH,
+        ).wait_recv()
+
+    def merge(t, u):
+        @pl.when(inner == 1)
+        def _():
+            wait_slot(t, u)
+
+            @pl.loop(0, BATCH)
+            def _(h):
+                both = parts[t, u, h].astype(jnp.float32) + slots[t, u, h].astype(jnp.float32)
+                parts[t, u, h] = both.astype(jnp.bfloat16)
+
+            z_copy(t, u).start()
+
+    def back(i, u):
+        peer = lax.rem(j + i, groups)
+        return pltpu.make_async_remote_copy(
+            src_ref=stage.at[u, :, rows_of(peer)],
+            dst_ref=out.at[pl.ds(u * BATCH, BATCH), mine],
+            send_sem=back_send.at[u, i - 1],
+            recv_sem=back_recv.at[u, i - 1],
+            device_id=(k, peer),
+            device_id_type=MESH,
+        )
+
+    def arrive_back(i, u):
+        peer = lax.rem(j + groups - i, groups)
+        return pltpu.make_async_remote_copy(
+            src_ref=stage.at[u, :, rows_of(peer)],
+            dst_ref=out.at[pl.ds(u * BATCH, BATCH), rows_of(peer)],
+            send_sem=back_send.at[u, i - 1],
+            recv_sem=back_recv.at[u, i - 1],
+            device_id=(k, peer),
+            device_id_type=MESH,
+        )
+
+    def keep_back(u):
+        return pltpu.make_async_copy(
+            stage.at[u, :, mine], out.at[pl.ds(u * BATCH, BATCH), mine], done_sem.at[u]
+        )
+
+    for n, (t, u) in enumerate(steps):
+        keep(n).wait()
+        for i in range(1, groups):
+            arrive_in(n, i).wait_recv()
+        if t == cuts - 1:
+            wait_slot(2, u)
+            wait_slot(3, u)
+
+        @pl.loop(0, BATCH // 2)
+        def _(m, n=n, t=t, u=u):
+            h = 2 * m
+            total = None
+            for s in range(slices):
+                term = rows_then_last(pair_of(land[n, s, h], land[n, s, h + 1]), s, 2)
+                total = term if total is None else total + term
+            for d in range(2):
+                rows = total[d * width : (d + 1) * width]
+                if t < cuts - 1:
+                    parts[t, u, h + d] = rows.astype(jnp.bfloat16)
+                else:
+                    for slot in (2, 3):
+                        rows = rows + slots[slot, u, h + d].astype(jnp.float32)
+                    stage[u, h + d] = rows.astype(jnp.bfloat16)
+
+        if t < 2:
+            @pl.when(outer == 1)
+            def _(t=t, u=u):
+                z_copy(t, u).start()
+        elif t == 2:
+            z_copy(t, u).start()
+        else:
+            for i in range(1, groups):
+                back(i, u).start()
+            keep_back(u).start()
+        if n >= LAG and steps[n - LAG][0] < 2:
+            merge(*steps[n - LAG])
+
+    for n in range(len(steps)):
+        for i in range(1, groups):
+            send_in(n, i).wait_send()
+    for t in range(cuts - 1):
+        for u in range(subs):
+            z_copy(t, u).wait_send()
+    for u in range(subs):
+        keep_back(u).wait()
+        for i in range(1, groups):
+            back(i, u).wait_send()
+    for u in range(subs):
+        for i in range(1, groups):
+            arrive_back(i, u).wait_recv()
+
+
+def per_device_fused(stem_state, gates):
+    cuts = lax.axis_size("cuts")
+    groups = lax.axis_size("amp")
+    slices, hidden, single, width, columns = stem_state.shape
+    share = hidden // cuts
+    subs = share // BATCH
+    steps = cuts * subs
+    bf16 = jnp.bfloat16
+    states = (steps, slices, BATCH, width, columns)
+    sums = (subs, BATCH, width, columns)
+    result = pl.pallas_call(
+        functools.partial(kernel, cuts, groups),
+        out_shape=jax.ShapeDtypeStruct((share, width, columns), bf16),
+        in_specs=[pl.BlockSpec(memory_space=pltpu.HBM)] * 2,
+        out_specs=pl.BlockSpec(memory_space=pl.ANY),
+        scratch_shapes=[
+            pltpu.VMEM(states, bf16),
+            pltpu.VMEM(gates.shape, bf16),
+            pltpu.VMEM((slices, 4, columns, columns), bf16),
+            pltpu.VMEM(states, bf16),
+            pltpu.VMEM(states, bf16),
+            pltpu.VMEM((cuts - 1,) + sums, bf16),
+            pltpu.VMEM((4,) + sums, bf16),
+            pltpu.VMEM(sums, bf16),
+            pltpu.SemaphoreType.DMA((steps, groups - 1)),
+            pltpu.SemaphoreType.DMA((steps, groups - 1)),
+            pltpu.SemaphoreType.DMA((cuts - 1, subs)),
+            pltpu.SemaphoreType.DMA((4, subs)),
+            pltpu.SemaphoreType.DMA((subs, groups - 1)),
+            pltpu.SemaphoreType.DMA((subs, groups - 1)),
+            pltpu.SemaphoreType.DMA((steps,)),
+            pltpu.SemaphoreType.DMA((steps,)),
+            pltpu.SemaphoreType.DMA,
+            pltpu.SemaphoreType.DMA((subs,)),
+        ],
+        compiler_params=pltpu.CompilerParams(
+            collective_id=0, has_side_effects=True, vmem_limit_bytes=60 * 1024 * 1024
+        ),
+    )(stem_state, gates)
+    return result.astype(jnp.float32).reshape(share, 1, width, columns)
+
+
+def per_device(stem_state, gates):
+    cuts = lax.axis_size("cuts")
+    groups = lax.axis_size("amp")
+    hidden, width = stem_state.shape[1], stem_state.shape[3]
+    if cuts == 4 and hidden % (cuts * BATCH) == 0 and width % (16 * groups) == 0:
+        return per_device_fused(stem_state, gates)
+    return per_device_general(stem_state, gates)
+
+
 def solution(mesh):
     placed = (P("cuts", None, "amp", None, None), P("cuts", None, None, None, None))
     return jax.shard_map(

time: 202 us -> 61.8 us (0.31)
  waiting for transfers between devices: 126 us -> 0 us
  Pallas kernels: 0 us -> 59.6 us
  matrix products: 21.1 us -> 0 us
  blocking collectives: 18.8 us -> 0 us
  between operations: 13.5 us -> 0.01 us
  local copies, waits for them, and re-layouts: 7.85 us -> 0 us
  other arithmetic: 8.68 us -> 2.11 us
  starting transfers between devices: 5.39 us -> 0 us
    reduce_scatter x1 -> x0, waiting for transfers between devices: 77.1 us -> none  [per_device(): summed = lax.psum_scatter(total, 'cuts', scatter_dimension=0, tiled=True)]
    pallas_call x0 -> x1, Pallas kernels: none -> 59.6 us  [per_device_fused(): pl.pallas_call(functools.partial(kernel, cuts, groups), out_shape=jax.Sha...]
    all_to_all x1 -> x0, waiting for transfers between devices: 48.8 us -> none  [per_device(): lax.all_to_all(split_state, 'amp', split_axis=3, concat_axis=2, tiled=True)]
    dot_general x6 -> x0, matrix products: 21.1 us -> none  [the longest x2 9.1 us: on_rows(): jnp.einsum('ska,shgac->shgkc', imag_gates, values, preferred_element_type...]
    all_to_all x1 -> x0, blocking collectives: 18.8 us -> none  [per_device(): lax.all_to_all(outgoing, 'amp', split_axis=1, concat_axis=2, tiled=True)]
    concatenate x2 -> x0, other arithmetic: 8.65 us -> none  [on_rows(): return jnp.concatenate([real_out, imag_out], axis=-1)]
    all_to_all x1 -> x0, starting transfers between devices: 5.17 us -> none  [per_device(): lax.all_to_all(split_state, 'amp', split_axis=3, concat_axis=2, tiled=True)]
    all_to_all x2 -> x0, local copies, waits for them, and re-layouts: 3.85 us -> none  [the longest x1 2.79 us: per_device(): lax.all_to_all(split_state, 'amp', split_axis=3, concat_axis=2, tiled=True)]
  transfers between devices with their start and end apart: 2 -> 0, of which waited for: 2 -> 0; matrix products, arithmetic and copies ran while one was open for 0% -> 0% of each run, Pallas kernels for 0% -> 0%
where the time goes in v3:
time: 61.8 us; the launch traced here: 61.7 us
  Pallas kernels  59.6 us (96%)
  other arithmetic  2.11 us (3%)
    pallas_call x1, Pallas kernels, per_device_fused(): pl.pallas_call(functools.partial(kernel, cuts, groups), out_shape=jax.Sha...  59.6 us
    reshape x1, other arithmetic, per_device_fused(): return result.astype(jnp.float32).reshape(share, 1, width, columns)  2.11 us

profile of v3, /device:TPU:0, one launch (start us, length us, event | category | flops | bytes accessed | tf_op | source)
XLA Modules:
  0.0 61.7 jit_solution(7431059709551209482)
XLA Ops:
  0.0 59.6 %shard_map.28 = bf16[8,128,256]{2,1,0:T(8,128)(2,1)} custom-call(bf16[2,32,1,128,256]{4,3,2,1,0:T(8,128)(2,1)} %stem.1, bf16[2,4,2,128,128]{4,3,2,1,0:T(8,128)(2,1)} %gates.1), custom_call_target="tpu_custom_call" | custom-call | tf_op jit(solution)/shard_map/pallas_call | solution.py:315
  59.6 2.1 %bitcast_convert_fusion = f32[8,1,128,256]{3,2,1,0:T(8,128)} fusion(bf16[8,128,256]{2,1,0:T(8,128)(2,1)} %shard_map.28), kind=kLoop, calls=%fused_computation | loop fusion | flops 262144 | bytes 1572864 | tf_op jit(solution)/shard_map/reshape | solution.py:344

commit v4 on v3

--- a/solution.py
+++ b/solution.py
@@ -9,7 +9,8 @@
 
 MESH = pl.DeviceIdType.MESH
 BATCH = 4
-LAG = 1
+FIRST = True
+FINAL = False
 
 
 def block_matrix(gate):
@@ -97,20 +98,21 @@
     inner = (k * (3 - k)) // 2
     outer = 1 - inner
     order = [3 * (1 - half), 2 - half, 4 * half + 1 - k, k]
-    steps = [(t, u) for t in range(cuts) for u in range(subs)]
+    steps = steps_of(cuts, share)
 
     def load(n):
-        t, u = steps[n]
+        t, at, size = steps[n]
         return pltpu.make_async_copy(
-            stem.at[:, pl.ds(order[t] * share + u * BATCH, BATCH), 0], stem_buf.at[n], stem_sem.at[n]
+            stem.at[:, pl.ds(order[t] * share + at, size), 0],
+            stem_buf.at[t, :, pl.ds(at, size)],
+            stem_sem.at[n],
         )
 
     for n in range(len(steps)):
         load(n).start()
 
-    gate_copy.wait()
-    for s in range(slices):
-        for n in range(4):
+    def prepare(n):
+        for s in range(slices):
             re = gate_buf[s, n, 0]
             im = gate_buf[s, n, 1]
             if n % 2 == 0:
@@ -126,6 +128,10 @@
                 blocks[s, n, width:, :width] = -im
                 blocks[s, n, width:, width:] = re
 
+    gate_copy.wait()
+    prepare(0)
+    prepare(1)
+
     def rows_then_last(pair, s, n):
         mid = dot(blocks[s, n], pair).astype(jnp.bfloat16)
         turned = jnp.concatenate(
@@ -140,11 +146,15 @@
     def rows_of(peer):
         return pl.ds(pl.multiple_of(peer * low, low), low)
 
+    def part_of(ref, n, rows):
+        t, at, size = steps[n]
+        return ref.at[t, :, pl.ds(at, size), rows]
+
     def send_in(n, i):
         peer = lax.rem(j + i, groups)
         return pltpu.make_async_remote_copy(
-            src_ref=second.at[n, :, :, rows_of(peer)],
-            dst_ref=land.at[n, :, :, mine],
+            src_ref=part_of(second, n, rows_of(peer)),
+            dst_ref=part_of(land, n, mine),
             send_sem=in_send.at[n, i - 1],
             recv_sem=in_recv.at[n, i - 1],
             device_id=(k, peer),
@@ -154,8 +164,8 @@
     def arrive_in(n, i):
         peer = lax.rem(j + groups - i, groups)
         return pltpu.make_async_remote_copy(
-            src_ref=land.at[n, :, :, rows_of(peer)],
-            dst_ref=land.at[n, :, :, rows_of(peer)],
+            src_ref=part_of(land, n, rows_of(peer)),
+            dst_ref=part_of(land, n, rows_of(peer)),
             send_sem=in_send.at[n, i - 1],
             recv_sem=in_recv.at[n, i - 1],
             device_id=(k, peer),
@@ -164,26 +174,29 @@
 
     def keep(n):
         return pltpu.make_async_copy(
-            second.at[n, :, :, mine], land.at[n, :, :, mine], own_sem.at[n]
-        )
-
-    for n in range(len(steps)):
+            part_of(second, n, mine), part_of(land, n, mine), own_sem.at[n]
+        )
+
+    for n, (t, at, size) in enumerate(steps):
         load(n).wait()
 
-        @pl.loop(0, BATCH // 2)
-        def _(m, n=n):
+        @pl.loop(at // 2, (at + size) // 2)
+        def _(m, t=t):
             h = 2 * m
             for s in range(slices):
-                res = rows_then_last(pair_of(stem_buf[n, s, h], stem_buf[n, s, h + 1]), s, 0)
+                res = rows_then_last(pair_of(stem_buf[t, s, h], stem_buf[t, s, h + 1]), s, 0)
                 res = res.astype(jnp.bfloat16)
-                second[n, s, h] = res[:width]
-                second[n, s, h + 1] = res[width:]
+                second[t, s, h] = res[:width]
+                second[t, s, h + 1] = res[width:]
 
         if n == 0:
             pl.semaphore_wait(barrier, groups - 1 + cuts - 1)
         for i in range(1, groups):
             send_in(n, i).start()
         keep(n).start()
+        if n == 0:
+            prepare(2)
+            prepare(3)
 
     def z_copy(t, u):
         if t < 2:
@@ -223,69 +236,80 @@
 
             z_copy(t, u).start()
 
-    def back(i, u):
+    last = [n for n in range(len(steps)) if steps[n][0] == cuts - 1]
+
+    def back(i, v):
+        at, size = steps[last[v]][1:]
         peer = lax.rem(j + i, groups)
         return pltpu.make_async_remote_copy(
-            src_ref=stage.at[u, :, rows_of(peer)],
-            dst_ref=out.at[pl.ds(u * BATCH, BATCH), mine],
-            send_sem=back_send.at[u, i - 1],
-            recv_sem=back_recv.at[u, i - 1],
+            src_ref=stage.at[pl.ds(at, size), rows_of(peer)],
+            dst_ref=out.at[pl.ds(at, size), mine],
+            send_sem=back_send.at[v, i - 1],
+            recv_sem=back_recv.at[v, i - 1],
             device_id=(k, peer),
             device_id_type=MESH,
         )
 
-    def arrive_back(i, u):
+    def arrive_back(i, v):
+        at, size = steps[last[v]][1:]
         peer = lax.rem(j + groups - i, groups)
         return pltpu.make_async_remote_copy(
-            src_ref=stage.at[u, :, rows_of(peer)],
-            dst_ref=out.at[pl.ds(u * BATCH, BATCH), rows_of(peer)],
-            send_sem=back_send.at[u, i - 1],
-            recv_sem=back_recv.at[u, i - 1],
+            src_ref=stage.at[pl.ds(at, size), rows_of(peer)],
+            dst_ref=out.at[pl.ds(at, size), rows_of(peer)],
+            send_sem=back_send.at[v, i - 1],
+            recv_sem=back_recv.at[v, i - 1],
             device_id=(k, peer),
             device_id_type=MESH,
         )
 
-    def keep_back(u):
+    def keep_back(v):
+        at, size = steps[last[v]][1:]
         return pltpu.make_async_copy(
-            stage.at[u, :, mine], out.at[pl.ds(u * BATCH, BATCH), mine], done_sem.at[u]
-        )
-
-    for n, (t, u) in enumerate(steps):
+            stage.at[pl.ds(at, size), mine], out.at[pl.ds(at, size), mine], done_sem.at[v]
+        )
+
+    waiting = []
+    for n, (t, at, size) in enumerate(steps):
         keep(n).wait()
         for i in range(1, groups):
             arrive_in(n, i).wait_recv()
-        if t == cuts - 1:
-            wait_slot(2, u)
-            wait_slot(3, u)
-
-        @pl.loop(0, BATCH // 2)
-        def _(m, n=n, t=t, u=u):
+        if t == cuts - 1 and at % BATCH == 0:
+            wait_slot(2, at // BATCH)
+            wait_slot(3, at // BATCH)
+
+        @pl.loop(at // 2, (at + size) // 2)
+        def _(m, t=t, u=at // BATCH):
             h = 2 * m
             total = None
             for s in range(slices):
-                term = rows_then_last(pair_of(land[n, s, h], land[n, s, h + 1]), s, 2)
+                term = rows_then_last(pair_of(land[t, s, h], land[t, s, h + 1]), s, 2)
                 total = term if total is None else total + term
             for d in range(2):
                 rows = total[d * width : (d + 1) * width]
                 if t < cuts - 1:
-                    parts[t, u, h + d] = rows.astype(jnp.bfloat16)
+                    parts[t, u, h + d - u * BATCH] = rows.astype(jnp.bfloat16)
                 else:
                     for slot in (2, 3):
-                        rows = rows + slots[slot, u, h + d].astype(jnp.float32)
-                    stage[u, h + d] = rows.astype(jnp.bfloat16)
-
-        if t < 2:
-            @pl.when(outer == 1)
-            def _(t=t, u=u):
+                        rows = rows + slots[slot, u, h + d - u * BATCH].astype(jnp.float32)
+                    stage[h + d] = rows.astype(jnp.bfloat16)
+
+        if t == cuts - 1:
+            v = last.index(n)
+            for i in range(1, groups):
+                back(i, v).start()
+            keep_back(v).start()
+        elif (at + size) % BATCH == 0:
+            u = at // BATCH
+            if t < 2:
+                @pl.when(outer == 1)
+                def _(t=t, u=u):
+                    z_copy(t, u).start()
+            else:
                 z_copy(t, u).start()
-        elif t == 2:
-            z_copy(t, u).start()
-        else:
-            for i in range(1, groups):
-                back(i, u).start()
-            keep_back(u).start()
-        if n >= LAG and steps[n - LAG][0] < 2:
-            merge(*steps[n - LAG])
+            if waiting:
+                merge(*waiting.pop())
+            if t < 2:
+                waiting.append((t, u))
 
     for n in range(len(steps)):
         for i in range(1, groups):
@@ -293,13 +317,22 @@
     for t in range(cuts - 1):
         for u in range(subs):
             z_copy(t, u).wait_send()
-    for u in range(subs):
-        keep_back(u).wait()
-        for i in range(1, groups):
-            back(i, u).wait_send()
-    for u in range(subs):
-        for i in range(1, groups):
-            arrive_back(i, u).wait_recv()
+    for v in range(len(last)):
+        keep_back(v).wait()
+        for i in range(1, groups):
+            back(i, v).wait_send()
+    for v in range(len(last)):
+        for i in range(1, groups):
+            arrive_back(i, v).wait_recv()
+
+
+def steps_of(cuts, share):
+    sizes = [[BATCH] * (share // BATCH) for t in range(cuts)]
+    if FIRST:
+        sizes[0][:1] = [BATCH // 2] * 2
+    if FINAL:
+        sizes[-1][-1:] = [BATCH // 2] * 2
+    return [(t, sum(row[:c]), row[c]) for t, row in enumerate(sizes) for c in range(len(row))]
 
 
 def per_device_fused(stem_state, gates):
@@ -308,9 +341,10 @@
     slices, hidden, single, width, columns = stem_state.shape
     share = hidden // cuts
     subs = share // BATCH
-    steps = cuts * subs
+    steps = len(steps_of(cuts, share))
+    last = len([step for step in steps_of(cuts, share) if step[0] == cuts - 1])
     bf16 = jnp.bfloat16
-    states = (steps, slices, BATCH, width, columns)
+    states = (cuts, slices, share, width, columns)
     sums = (subs, BATCH, width, columns)
     result = pl.pallas_call(
         functools.partial(kernel, cuts, groups),
@@ -325,17 +359,17 @@
             pltpu.VMEM(states, bf16),
             pltpu.VMEM((cuts - 1,) + sums, bf16),
             pltpu.VMEM((4,) + sums, bf16),
-            pltpu.VMEM(sums, bf16),
+            pltpu.VMEM((share, width, columns), bf16),
             pltpu.SemaphoreType.DMA((steps, groups - 1)),
             pltpu.SemaphoreType.DMA((steps, groups - 1)),
             pltpu.SemaphoreType.DMA((cuts - 1, subs)),
             pltpu.SemaphoreType.DMA((4, subs)),
-            pltpu.SemaphoreType.DMA((subs, groups - 1)),
-            pltpu.SemaphoreType.DMA((subs, groups - 1)),
+            pltpu.SemaphoreType.DMA((last, groups - 1)),
+            pltpu.SemaphoreType.DMA((last, groups - 1)),
             pltpu.SemaphoreType.DMA((steps,)),
             pltpu.SemaphoreType.DMA((steps,)),
             pltpu.SemaphoreType.DMA,
-            pltpu.SemaphoreType.DMA((subs,)),
+            pltpu.SemaphoreType.DMA((last,)),
         ],
         compiler_params=pltpu.CompilerParams(
             collective_id=0, has_side_effects=True, vmem_limit_bytes=60 * 1024 * 1024

time: 61.8 us -> 61.9 us (level)
  no operation moved by 1% of the time
where the time goes in v4:
time: 61.9 us; the launch traced here: 61.8 us
  Pallas kernels  59.7 us (96%)
  other arithmetic  2.11 us (3%)
    pallas_call x1, Pallas kernels, per_device_fused(): pl.pallas_call(functools.partial(kernel, cuts, groups), out_shape=jax.Sha...  59.7 us
    reshape x1, other arithmetic, per_device_fused(): return result.astype(jnp.float32).reshape(share, 1, width, columns)  2.11 us

profile of v4, /device:TPU:0, one launch (start us, length us, event | category | flops | bytes accessed | tf_op | source)
XLA Modules:
  0.0 61.8 jit_solution(12276155852780285604)
XLA Ops:
  0.0 59.7 %shard_map.28 = bf16[8,128,256]{2,1,0:T(8,128)(2,1)} custom-call(bf16[2,32,1,128,256]{4,3,2,1,0:T(8,128)(2,1)} %stem.1, bf16[2,4,2,128,128]{4,3,2,1,0:T(8,128)(2,1)} %gates.1), custom_call_target="tpu_custom_call" | custom-call | tf_op jit(solution)/shard_map/pallas_call | solution.py:349
  59.7 2.1 %bitcast_convert_fusion = f32[8,1,128,256]{3,2,1,0:T(8,128)} fusion(bf16[8,128,256]{2,1,0:T(8,128)(2,1)} %shard_map.28), kind=kLoop, calls=%fused_computation | loop fusion | flops 262144 | bytes 1572864 | tf_op jit(solution)/shard_map/reshape | solution.py:378
